TPU v7x, 32 devices: a whole 2x2x4 slice. The times are simulated.
32 devices in a mesh: groups: 2 (over y), seq: 16 (over z, x, core).
Axes of the slice: x: 2, y: 2, z: 4, core: 2. Of those that a mesh axis runs over, the one named last changes fastest.
Arguments:
- queries: bfloat16 [4096, 2048], P(('groups', 'seq')), parts along dimension 0, may hold values from -240 to 240, as said below
- encodings: bfloat16 [64, 128, 1024], P('groups', 'seq'), parts along dimension 0, may hold values from -6 to 6
- neighbour_ids: int32 [64, 2], P(('groups', 'seq')), parts along dimension 0, may hold values from 0 to 31
- lengths: int32 [4], P('groups'), parts along dimension 0, may hold values from 64 to 1024, as said below
- w_key: bfloat16 [1024, 2048], replicated, may hold values from -0.1875 to 0.1875
- w_value: bfloat16 [1024, 2048], replicated, may hold values from -0.1875 to 0.1875
Outputs:
- attended: bfloat16 [4096, 2048], P(('groups', 'seq')), parts along dimension 0
There are 2 independent parts, one for each index of `groups`. A program takes and returns all parts, laid end to end along the dimension named above; an argument that names none is the same for every part. Nothing has to cross between parts.
Inputs may be any that keep to these rules, and one draw needn't show every extreme that they name: `queries`: queries are of order one in the shown draw; rows may have unlike scales. `lengths`: each length is a multiple of nothing in particular; some prompt fills its room of 1024 tokens.
All inputs are finite; a program needn't handle non-finite values.
Results may differ from a plain program's by a relative error of at most 0.012.
The roundings to bfloat16 on the way count: a program that leaves them out, or rounds other values in their place, can miss the bound.
Values may be sent and summed in bfloat16 or wider, within the bound.
A program may use at most 64 MiB of HBM per device.

v0:
```python
import jax
import jax.numpy as jnp
from jax import lax
from jax.sharding import PartitionSpec as P

HEADS = 16
DH = 128


def body(queries, encodings, neighbour_ids, lengths, w_key, w_value):
    seq_count = lax.axis_size("seq")
    position = lax.axis_index("seq")
    tok_rows, width = queries.shape
    blocks = tok_rows // 64
    slots = blocks + 1
    enc_width = encodings.shape[2]
    id_all = lax.all_gather(neighbour_ids, "seq", axis=0, tiled=True)
    total_spans = id_all.shape[0]
    wanted_span = (
        jnp.arange(seq_count, dtype=jnp.int32)[:, None] * blocks
        - 1
        + jnp.arange(slots, dtype=jnp.int32)[None, :]
    )
    wanted_span = jnp.clip(wanted_span, 0, total_spans - 1)
    wanted = id_all[wanted_span].reshape(seq_count, 2 * slots)
    outgoing = encodings[wanted]
    block = lax.all_to_all(outgoing, "seq", split_axis=0, concat_axis=2, tiled=True)
    flat = block.reshape(-1, enc_width)
    shape = block.shape[:3] + (width,)
    key_rows = (
        jnp.dot(flat, w_key, preferred_element_type=jnp.float32).astype(jnp.bfloat16).reshape(shape)
    )
    value_rows = (
        jnp.dot(flat, w_value, preferred_element_type=jnp.float32)
        .astype(jnp.bfloat16)
        .reshape(shape)
    )
    ntok = key_rows.shape[2]
    key_total = key_rows.shape[1] * ntok
    key_set = key_rows.reshape(key_total, HEADS, DH)
    value_set = value_rows.reshape(key_total, HEADS, DH)
    key_slot = jnp.arange(key_total, dtype=jnp.int32) // (2 * ntok)
    local_rows = jnp.arange(tok_rows, dtype=jnp.int32)
    token_slot = (local_rows + 1) // 64
    allowed = token_slot[:, None] == key_slot[None, :]
    query_set = queries.reshape(tok_rows, HEADS, DH)
    scale = 1.0 / DH**0.5
    scores = (
        jnp.einsum("thd,khd->htk", query_set, key_set, preferred_element_type=jnp.float32) * scale
    )
    scores = jnp.where(allowed[None, :, :], scores, -1e30)
    top = jnp.max(scores, axis=2, keepdims=True)
    expo = jnp.where(allowed[None, :, :], jnp.exp(scores - top), 0.0)
    weights = (expo / jnp.sum(expo, axis=2, keepdims=True)).astype(jnp.bfloat16)
    result = jnp.einsum(
        "htk,khd->thd", weights, value_set, preferred_element_type=jnp.float32
    ).reshape(tok_rows, width)
    slot_room = tok_rows * seq_count // lengths.shape[0]
    global_rows = position * tok_rows + local_rows
    within = global_rows % slot_room
    prompt = global_rows // slot_room
    limit = jnp.sum(
        jnp.where(
            prompt[:, None] == jnp.arange(lengths.shape[0], dtype=jnp.int32)[None, :],
            lengths[None, :],
            0,
        ),
        axis=1,
    )
    live = (within >= 63) & (within < limit)
    return jnp.where(live[:, None], result, 0.0).astype(jnp.bfloat16)


def solution(mesh):
    in_specs = (
        P(("groups", "seq"), None),
        P("groups", "seq", None),
        P(("groups", "seq"), None),
        P("groups"),
        P(),
        P(),
    )
    out_specs = P(("groups", "seq"), None)
    return jax.shard_map(body, mesh=mesh, in_specs=in_specs, out_specs=out_specs, check_vma=False)
```

profile of v0, /device:TPU:11, one launch (start us, length us, event | category | flops | bytes accessed | tf_op | source)
XLA Modules:
  0.0 91.5 jit_solution(18031482565130279653)
XLA Ops:
  0.0 0.0 copy-start
  0.0 0.0 copy-start.3
  0.0 16.0 %all-gather = s32[16,2,2]{2,1,0:T(2,128)S(1)} all-gather(s32[1,2,2]{2,1,0:T(2,128)} %bitcast.50), channel_id=1, replica_groups=mesh['groups'=2,'seq'=16] {'seq'}, dimensions={0}, use_global_device_ids=true | all-gather | bytes 272 | tf_op jit(solution)/shard_map/all_gather | solution.py:17
  16.0 0.1 compare_select_fusion.1
  16.1 0.1 reshape.195
  16.2 0.6 gather_fusion
  16.8 0.1 reshape.189
  16.9 0.1 reshape.203
  17.0 3.0 %gather_fusion.1 = bf16[96,8,1024]{2,1,0:T(8,128)(2,1)} fusion(bf16[32,8,1024]{2,1,0:T(8,128)(2,1)} %param.7, s32[1024]{0:T(1024)S(1)} %pad_clamp_fusion), kind=kCustom, calls=%fused_computation.1 | custom fusion | bytes 3146112 | tf_op jit(solution)/shard_map/gather | solution.py:26
  19.9 10.3 %all-to-all-start = ((bf16[16,6,8,1024]{3,2,1,0:T(8,128)(2,1)}), bf16[16,6,8,1024]{3,2,1,0:T(8,128)(2,1)S(1)}, u32[]{:S(2)}, u32[]{:S(2)}) async-start(bf16[16,6,8,1024]{3,2,1,0:T(8,128)(2,1)} %bitcast.44), calls=%async_computation | async-start | bytes 3145728 | tf_op jit(solution)/shard_map/all_to_all | solution.py:27
  30.2 0.0 copy-done.3
  30.2 0.1 fusion.15
  30.3 0.2 broadcast_compare_fusion
  30.5 35.9 %all-to-all-done = bf16[16,6,8,1024]{3,2,1,0:T(8,128)(2,1)S(1)} async-done(((bf16[16,6,8,1024]{3,2,1,0:T(8,128)(2,1)}), bf16[16,6,8,1024]{3,2,1,0:T(8,128)(2,1)S(1)}, u32[]{:S(2)}, u32[]{:S(2)}) %all-to-all-start) | async-done | bytes 1572896 | tf_op jit(solution)/shard_map/all_to_all | solution.py:27
  66.4 0.1 copy.39
  66.5 0.0 copy-start.2
  66.6 7.1 %fusion.9 = bf16[96,16,8,128]{3,2,1,0:T(8,128)(2,1)} fusion(bf16[768,1024]{1,0:T(8,128)(2,1)S(1)} %bitcast.47, bf16[1024,2048]{1,0:T(8,128)(2,1)} %param.10), kind=kOutput, calls=%fused_computation.16 | convolution fusion | flops 3222798336 | bytes 8912896 | tf_op jit(solution)/shard_map/dot_general | solution.py:31
  73.7 0.0 copy-done.2
  73.7 4.8 %convolution_convert_fusion.1 = bf16[768,2048]{1,0:T(8,128)(2,1)} fusion(bf16[768,1024]{1,0:T(8,128)(2,1)S(1)} %bitcast.48, bf16[1024,2048]{1,0:T(8,128)(2,1)S(1)} %copy-done.2), kind=kOutput, calls=%fused_computation.8 | convolution fusion | flops 3222798336 | bytes 8912896 | tf_op jit(solution)/shard_map/dot_general | solution.py:34
  78.5 4.7 %copy.47 = bf16[768,2048]{0,1:T(8,128)(2,1)} copy(bf16[768,2048]{1,0:T(8,128)(2,1)} %convolution_convert_fusion.1) | data formatting | bytes 6291456 | tf_op jit(solution)/shard_map/reshape;reshape | solution.py:41
  83.2 0.0 copy-done
  83.2 2.9 %fusion.2 = f32[16,768,128]{2,1,0:T(8,128)S(1)} fusion(bf16[96,16,8,128]{3,2,1,0:T(8,128)(2,1)} %fusion.9, bf16[128,2048]{1,0:T(8,128)(2,1)S(1)} %copy-done), kind=kOutput, calls=%fused_computation.9 | convolution fusion | flops 402653184 | bytes 9961472 | tf_op jit(solution)/shard_map/thd,khd->htk/dot_general | solution.py:49
  86.1 0.0 copy-start.1
  86.1 3.2 %fusion.18 = (f32[16,128]{1,0:T(8,128)S(1)}, f32[16,128,768]{1,2,0:T(8,128)S(1)}) fusion(f32[16,768,128]{2,1,0:T(8,128)S(1)} %fusion.2, pred[128,768]{0,1:T(8,128)(4,1)S(1)} %broadcast_compare_fusion), kind=kOutput, calls=%fused_computation.48 | output fusion | flops 11010815 | bytes 12689408 | tf_op jit(solution)/shard_map/sub | solution.py:53
  89.3 0.0 copy-done.1
  89.3 1.0 %fusion.7 = bf16[16,128,128]{2,1,0:T(8,128)(2,1)S(1)} fusion(bf16[768,16,128]{0,2,1:T(8,128)(2,1)S(1)} %bitcast.46, f32[16,128,768]{1,2,0:T(8,128)S(1)} %get-tuple-element.6, f32[16,128]{1,0:T(8,128)S(1)} %get-tuple-element.5), kind=kOutput, calls=%fused_computation.14 | convolution fusion | flops 405798912 | bytes 9969664 | tf_op jit(solution)/shard_map/htk,khd->thd/dot_general | solution.py:55
  90.3 0.2 copy.44
  90.6 1.0 %select_convert_fusion = bf16[128,2048]{1,0:T(8,128)(2,1)} fusion(bf16[128,2048]{1,0:T(8,128)(2,1)S(1)} %copy.44, pred[128]{0:T(512)(128)(4,1)S(1)} %compare_and_fusion), kind=kLoop, calls=%fused_computation.17 | loop fusion | flops 262144 | bytes 1048704 | tf_op jit(solution)/shard_map/convert_element_type | solution.py:71
  (8 shorter events, 0.1 us)
Async XLA Ops:
  0.0 83.2 %copy-start = (bf16[128,2048]{1,0:T(8,128)(2,1)S(1)}, bf16[128,2048]{1,0:T(8,128)(2,1)}, u32[]{:S(2)}) copy-start(bf16[128,2048]{1,0:T(8,128)(2,1)} %param.6) | copy-start | bytes 1572868
  0.0 30.2 %copy-start.3 = (s32[2]{0:T(128)S(1)}, s32[2]{0:T(128)}, u32[]{:S(2)}) copy-start(s32[2]{0:T(128)} %param.9) | copy-start | bytes 28
  19.9 46.5 %all-to-all-start = ((bf16[16,6,8,1024]{3,2,1,0:T(8,128)(2,1)}), bf16[16,6,8,1024]{3,2,1,0:T(8,128)(2,1)S(1)}, u32[]{:S(2)}, u32[]{:S(2)}) async-start(bf16[16,6,8,1024]{3,2,1,0:T(8,128)(2,1)} %bitcast.44), calls=%async_computation | async-start | bytes 3145728 | tf_op jit(solution)/shard_map/all_to_all | solution.py:27
  66.5 7.1 %copy-start.2 = (bf16[1024,2048]{1,0:T(8,128)(2,1)S(1)}, bf16[1024,2048]{1,0:T(8,128)(2,1)}, u32[]{:S(2)}) copy-start(bf16[1024,2048]{1,0:T(8,128)(2,1)} %param.11) | copy-start | bytes 12582916
  86.1 3.3 %copy-start.1 = (bf16[768,2048]{0,1:T(8,128)(2,1)S(1)}, bf16[768,2048]{0,1:T(8,128)(2,1)}, u32[]{:S(2)}) copy-start(bf16[768,2048]{0,1:T(8,128)(2,1)} %copy.47) | copy-start | bytes 9437188
where the time goes:
time: 91.9 us; the launch traced here: 91.5 us
  waiting for transfers between devices  35.9 us (39%)
  blocking collectives  16 us (17%)
  matrix products  15.8 us (17%)
  starting transfers between devices  10.3 us (11%)
  local copies, waits for them, and re-layouts  8.86 us (10%)
  other arithmetic  4.59 us (5%)
    all_to_all x1, waiting for transfers between devices, body(): lax.all_to_all(outgoing, 'seq', split_axis=0, concat_axis=2, tiled=True)  35.9 us
    all_gather x1, blocking collectives, body(): id_all = lax.all_gather(neighbour_ids, 'seq', axis=0, tiled=True)  16 us
    all_to_all x1, starting transfers between devices, body(): lax.all_to_all(outgoing, 'seq', split_axis=0, concat_axis=2, tiled=True)  10.3 us
    dot_general x1, matrix products, body(): jnp.dot(flat, w_key, preferred_element_type=jnp.float32)  7.11 us
    dot_general x1, matrix products, body(): jnp.dot(flat, w_value, preferred_element_type=jnp.float32)  4.83 us
    another operation x1, local copies, waits for them, and re-layouts, body(): value_set = value_rows.reshape(key_total, HEADS, DH)  4.69 us
    sub x1, other arithmetic, body(): expo = jnp.where(allowed[None, :, :], jnp.exp(scores - top), 0.0)  3.25 us
    gather x1, local copies, waits for them, and re-layouts, body(): outgoing = encodings[wanted]  2.95 us
  transfers between devices with their start and end apart: 1, of which 1 were waited for; matrix products, arithmetic and copies ran while one was open for 0% of the time, Pallas kernels for 0%

commit v1 on v0

--- a/solution.py
+++ b/solution.py
@@ -1,13 +1,17 @@
+import functools
 import jax
 import jax.numpy as jnp
 from jax import lax
+from jax.experimental import pallas as pl
+from jax.experimental.pallas import tpu as pltpu
 from jax.sharding import PartitionSpec as P
 
 HEADS = 16
 DH = 128
-
-
-def body(queries, encodings, neighbour_ids, lengths, w_key, w_value):
+SPAN = 64
+
+
+def general_body(queries, encodings, neighbour_ids, lengths, w_key, w_value):
     seq_count = lax.axis_size("seq")
     position = lax.axis_index("seq")
     tok_rows, width = queries.shape
@@ -71,6 +75,286 @@
     return jnp.where(live[:, None], result, 0.0).astype(jnp.bfloat16)
 
 
+def flipped(index, offset):
+    bit = 1
+    while bit <= offset:
+        if offset & bit:
+            index = index + bit - 2 * bit * ((index // bit) % 2)
+        bit *= 2
+    return index
+
+
+def kernel(
+    count,
+    toks,
+    ids_ref,
+    q_ref,
+    enc_hbm,
+    wk_hbm,
+    wv_hbm,
+    out_ref,
+    enc_ref,
+    wk_ref,
+    wv_ref,
+    id_send,
+    id_recv,
+    send_buf,
+    recv_buf,
+    q_send,
+    q_recv,
+    q_shift,
+    k_buf,
+    v_buf,
+    result,
+    row_send,
+    row_recv,
+    local_sem,
+    id_ssem,
+    id_rsem,
+    x_ssem,
+    x_rsem,
+    row_ssem,
+    row_rsem,
+):
+    me = lax.axis_index("seq")
+    following = lax.rem(me + 1, count)
+    previous = lax.rem(me + count - 1, count)
+    rows = 2 * toks
+    total = count * rows
+    enc_width = enc_ref.shape[1]
+    width = q_ref.shape[1]
+    offsets = sorted(range(1, count), reverse=True)
+
+    def local(source, target, index):
+        copy = pltpu.make_async_copy(source, target, local_sem.at[index])
+        copy.start()
+        return copy
+
+    def remote(source, target, send_sem, recv_sem, device):
+        return pltpu.make_async_remote_copy(
+            src_ref=source,
+            dst_ref=target,
+            send_sem=send_sem,
+            recv_sem=recv_sem,
+            device_id={"seq": device},
+            device_id_type=pl.DeviceIdType.MESH,
+        )
+
+    barrier = pltpu.get_barrier_semaphore()
+    for offset in offsets:
+        pl.semaphore_signal(
+            barrier,
+            inc=1,
+            device_id={"seq": flipped(me, offset)},
+            device_id_type=pl.DeviceIdType.MESH,
+        )
+    enc_copy = local(enc_hbm, enc_ref, 0)
+    wk_copy = local(wk_hbm, wk_ref, 1)
+    wv_copy = local(wv_hbm, wv_ref, 2)
+
+    lane = lax.broadcasted_iota(jnp.int32, (1, 128), 1)
+    mine = jnp.zeros((1, 128), jnp.float32)
+    for span in range(2):
+        for which in range(2):
+            value = ids_ref[span, which].astype(jnp.float32)
+            mine = jnp.where(lane == me * 4 + span * 2 + which, value, mine)
+    id_send[...] = mine
+    id_recv[me] = mine
+    last = q_ref.shape[0] - 1
+    q_send[...] = q_ref[last - 15 :, :].astype(jnp.float32)[15:, :]
+
+    pl.semaphore_wait(barrier, count - 1)
+
+    id_copies = {}
+    for offset in offsets:
+        id_copies[offset] = remote(
+            id_send, id_recv.at[me], id_ssem.at[offset], id_rsem.at[offset], flipped(me, offset)
+        )
+        id_copies[offset].start()
+    q_copy = remote(q_send, q_recv, row_ssem.at[0], row_rsem.at[0], following)
+    q_copy.start()
+    enc_copy.wait()
+    for offset in offsets:
+        id_copies[offset].wait_recv()
+    ids = jnp.sum(id_recv[...], axis=0)
+
+    x_copies = {}
+    for slot in range(2):
+        row = lax.broadcasted_iota(jnp.int32, (total, 128), 0)
+        lanes = lax.broadcasted_iota(jnp.int32, (total, 128), 1)
+        peer = row // rows
+        which = (row % rows) // toks
+        if slot == 0:
+            origin = lax.rem(peer + count - 1, count) * 4 + 2 + which
+        else:
+            origin = peer * 4 + which
+        chosen = jnp.sum(
+            jnp.where(lanes == origin, jnp.broadcast_to(ids, (total, 128)), 0.0),
+            axis=1,
+            keepdims=True,
+        )
+        held = enc_ref.shape[0]
+        tok = (lax.broadcasted_iota(jnp.int32, (total, held), 0) % toks).astype(jnp.float32)
+        column = lax.broadcasted_iota(jnp.int32, (total, held), 1).astype(jnp.float32)
+        pick = jnp.where(column == chosen * toks + tok, 1.0, 0.0).astype(jnp.bfloat16)
+        for part in range(enc_width // 256):
+            cols = slice(part * 256, part * 256 + 256)
+            send_buf[slot, :, cols] = jnp.dot(
+                pick, enc_ref[:, cols], preferred_element_type=jnp.float32
+            ).astype(jnp.bfloat16)
+        own = pl.ds(pl.multiple_of(me * rows, rows), rows)
+        for offset in offsets:
+            peer_at = flipped(me, offset)
+            theirs = pl.ds(pl.multiple_of(peer_at * rows, rows), rows)
+            copy = remote(
+                send_buf.at[slot, theirs],
+                recv_buf.at[slot, own],
+                x_ssem.at[slot, offset],
+                x_rsem.at[slot, offset],
+                peer_at,
+            )
+            copy.start()
+            x_copies[slot, offset] = copy
+        recv_buf[slot, own, :] = send_buf[slot, own, :]
+
+    q_copy.wait_recv()
+    for part in range(width // 256):
+        cols = slice(part * 256, part * 256 + 256)
+        turned = pltpu.roll(q_ref[:, cols].astype(jnp.float32), 1, 0)
+        first = lax.broadcasted_iota(jnp.int32, turned.shape, 0) == 0
+        turned = jnp.where(first, jnp.broadcast_to(q_recv[:, cols], turned.shape), turned)
+        q_shift[:, cols] = turned.astype(jnp.bfloat16)
+    wk_copy.wait()
+    wv_copy.wait()
+
+    scale = 1.0 / DH**0.5
+    for slot in range(2):
+        for offset in offsets:
+            x_copies[slot, offset].wait_recv()
+
+        @pl.loop(0, width // 256)
+        def project(tile):
+            cols = pl.ds(pl.multiple_of(tile * 256, 256), 256)
+            x = recv_buf[slot]
+            k_buf[:, cols] = jnp.dot(
+                x, wk_ref[:, cols], preferred_element_type=jnp.float32
+            ).astype(jnp.bfloat16)
+            v_buf[:, cols] = jnp.dot(
+                x, wv_ref[:, cols], preferred_element_type=jnp.float32
+            ).astype(jnp.bfloat16)
+
+        @pl.loop(0, HEADS // 4)
+        def attend(step):
+            for part in range(4):
+                cols = pl.ds(pl.multiple_of((step * 4 + part) * DH, DH), DH)
+                query = q_shift[slot * SPAN : slot * SPAN + SPAN, cols]
+                scores = (
+                    lax.dot_general(
+                        query,
+                        k_buf[:, cols],
+                        (((1,), (1,)), ((), ())),
+                        preferred_element_type=jnp.float32,
+                    )
+                    * scale
+                )
+                top = jnp.max(scores, axis=1, keepdims=True)
+                expo = jnp.exp(scores - top)
+                weights = (expo / jnp.sum(expo, axis=1, keepdims=True)).astype(jnp.bfloat16)
+                result[pl.ds(7 + slot * SPAN, SPAN), cols] = jnp.dot(
+                    weights, v_buf[:, cols], preferred_element_type=jnp.float32
+                )
+
+        if slot == 0:
+            row_send[...] = result[7:8, :]
+            row_copy = remote(row_send, row_recv, row_ssem.at[1], row_rsem.at[1], previous)
+            row_copy.start()
+
+    row_copy.wait_recv()
+    result[8 + last : 9 + last, :] = row_recv[...]
+    out_ref[...] = result[8 : 9 + last, :].astype(jnp.bfloat16)
+    for offset in offsets:
+        id_copies[offset].wait_send()
+        for slot in range(2):
+            x_copies[slot, offset].wait_send()
+    q_copy.wait_send()
+    row_copy.wait_send()
+
+
+def kernel_body(queries, encodings, neighbour_ids, lengths, w_key, w_value):
+    count = lax.axis_size("seq")
+    position = lax.axis_index("seq")
+    tok_rows, width = queries.shape
+    held, toks, enc_width = encodings.shape
+    total = count * 2 * toks
+    dma = pltpu.SemaphoreType.DMA
+    attended = pl.pallas_call(
+        functools.partial(kernel, count, toks),
+        out_shape=jax.ShapeDtypeStruct((tok_rows, width), jnp.bfloat16),
+        in_specs=[
+            pl.BlockSpec(memory_space=pltpu.SMEM),
+            pl.BlockSpec(memory_space=pltpu.VMEM),
+            pl.BlockSpec(memory_space=pl.ANY),
+            pl.BlockSpec(memory_space=pl.ANY),
+            pl.BlockSpec(memory_space=pl.ANY),
+        ],
+        out_specs=pl.BlockSpec(memory_space=pltpu.VMEM),
+        scratch_shapes=[
+            pltpu.VMEM((held * toks, enc_width), jnp.bfloat16),
+            pltpu.VMEM((enc_width, width), jnp.bfloat16),
+            pltpu.VMEM((enc_width, width), jnp.bfloat16),
+            pltpu.VMEM((1, 128), jnp.float32),
+            pltpu.VMEM((count, 1, 128), jnp.float32),
+            pltpu.VMEM((2, total, enc_width), jnp.bfloat16),
+            pltpu.VMEM((2, total, enc_width), jnp.bfloat16),
+            pltpu.VMEM((1, width), jnp.float32),
+            pltpu.VMEM((1, width), jnp.float32),
+            pltpu.VMEM((tok_rows, width), jnp.bfloat16),
+            pltpu.VMEM((total, width), jnp.bfloat16),
+            pltpu.VMEM((total, width), jnp.bfloat16),
+            pltpu.VMEM((tok_rows + 8, width), jnp.float32),
+            pltpu.VMEM((1, width), jnp.float32),
+            pltpu.VMEM((1, width), jnp.float32),
+            dma((3,)),
+            dma((count,)),
+            dma((count,)),
+            dma((2, count)),
+            dma((2, count)),
+            dma((2,)),
+            dma((2,)),
+        ],
+        compiler_params=pltpu.CompilerParams(
+            collective_id=0, has_side_effects=True, vmem_limit_bytes=48 * 1024 * 1024
+        ),
+        cost_estimate=pl.CostEstimate(
+            flops=8 * total * enc_width * width, bytes_accessed=10 << 20, transcendentals=0
+        ),
+    )(neighbour_ids, queries, encodings.reshape(held * toks, enc_width), w_key, w_value)
+    slot_room = tok_rows * count // lengths.shape[0]
+    global_rows = position * tok_rows + jnp.arange(tok_rows, dtype=jnp.int32)
+    within = global_rows % slot_room
+    prompt = global_rows // slot_room
+    limit = jnp.sum(
+        jnp.where(
+            prompt[:, None] == jnp.arange(lengths.shape[0], dtype=jnp.int32)[None, :],
+            lengths[None, :],
+            0,
+        ),
+        axis=1,
+    )
+    live = (within >= 63) & (within < limit)
+    return jnp.where(live[:, None], attended, 0).astype(jnp.bfloat16)
+
+
+def body(queries, encodings, neighbour_ids, lengths, w_key, w_value):
+    count = lax.axis_size("seq")
+    held, toks, enc_width = encodings.shape
+    small = count <= 32 and count & (count - 1) == 0 and held <= 256
+    tiled = (2 * toks) % 16 == 0 and (held * toks) % 16 == 0
+    if small and tiled and queries.shape[0] == 2 * SPAN:
+        return kernel_body(queries, encodings, neighbour_ids, lengths, w_key, w_value)
+    return general_body(queries, encodings, neighbour_ids, lengths, w_key, w_value)
+
+
 def solution(mesh):
     in_specs = (
         P(("groups", "seq"), None),

time: 91.9 us -> 56.5 us (0.61)
  the two profiles are of different devices: /device:TPU:11 before, /device:TPU:0 now
where the time goes in v1:
time: 56.5 us; the launch traced here: 56.2 us
  Pallas kernels  49.6 us (88%)
  local copies, waits for them, and re-layouts  4.94 us (9%)
  other arithmetic  1.67 us (3%)
    pallas_call x1, Pallas kernels, kernel_body(): pl.pallas_call(functools.partial(kernel, count, toks), out_shape=jax.Shap...  49.6 us
    unnamed x8, local copies, waits for them, and re-layouts  4.94 us

profile of v1, /device:TPU:0, one launch (start us, length us, event | category | flops | bytes accessed | tf_op | source)
XLA Modules:
  0.0 56.2 jit_solution(10940361239313485815)
XLA Ops:
  0.0 0.7 %fusion = s32[128]{0:T(128)S(1)} fusion(s32[2]{0:T(128)} %param.9, s32[128]{0:T(128)S(1)} %and_select_fusion), kind=kLoop, calls=%fused_computation.8 | loop fusion | flops 640 | bytes 1032 | tf_op jit(solution)/shard_map/reduce_sum | solution.py:336
  0.8 0.0 copy-start
  0.8 2.2 %copy-done = bf16[1024,2048]{1,0:T(8,128)(2,1)S(1)} copy-done((bf16[1024,2048]{1,0:T(8,128)(2,1)S(1)}, bf16[1024,2048]{1,0:T(8,128)(2,1)}, u32[]{:S(2)}) %copy-start) | copy-done | bytes 4194328
  3.0 0.0 copy-start.1
  3.0 1.0 %copy-done.1 = bf16[128,2048]{1,0:T(8,128)(2,1)S(1)} copy-done((bf16[128,2048]{1,0:T(8,128)(2,1)S(1)}, bf16[128,2048]{1,0:T(8,128)(2,1)}, u32[]{:S(2)}) %copy-start.1) | copy-done | bytes 524312
  4.0 0.0 copy-start.2
  4.0 1.0 %copy-done.2 = bf16[32,8,1024]{2,1,0:T(8,128)(2,1)S(1)} copy-done((bf16[32,8,1024]{2,1,0:T(8,128)(2,1)S(1)}, bf16[32,8,1024]{2,1,0:T(8,128)(2,1)}, u32[]{:S(2)}) %copy-start.2) | copy-done | bytes 524312
  5.0 0.0 copy-start.3
  5.0 0.7 %copy-done.3 = s32[2,2]{1,0:T(2,128)S(1)} copy-done((s32[2,2]{1,0:T(2,128)S(1)}, s32[2,2]{1,0:T(2,128)}, u32[]{:S(2)}) %copy-start.3) | copy-done | bytes 40
  5.7 49.6 %shard_map.64 = bf16[128,2048]{1,0:T(8,128)(2,1)S(1)} custom-call(s32[2,2]{1,0:T(2,128)S(1)} %copy-done.3, bf16[128,2048]{1,0:T(8,128)(2,1)S(1)} %copy-done.1, bf16[256,1024]{1,0:T(8,128)(2,1)S(1)} %bitcast.1, bf16[1024,2048]{1,0:T(8,128)(2,1)S(1)} %copy-done, bf16[1024,2048]{1,0:T(8,128)(2,1)} %wv_hbm.1), custom_call_target="tpu_custom_call" | custom-call | flops 4294967296 | bytes 10485760 | tf_op jit(solution)/shard_map/pallas_call | solution.py:290
  55.3 0.9 %broadcast_select_fusion = bf16[128,2048]{1,0:T(8,128)(2,1)} fusion(bf16[128,2048]{1,0:T(8,128)(2,1)S(1)} %shard_map.64, pred[128]{0:T(512)(128)(4,1)S(1)} %compare_and_fusion), kind=kLoop, calls=%fused_computation | loop fusion | flops 262144 | bytes 1048704 | tf_op jit(solution)/shard_map/jit(_where)/select_n | solution.py:345
  (2 shorter events, 0.0 us)
Async XLA Ops:
  0.8 2.2 %copy-start = (bf16[1024,2048]{1,0:T(8,128)(2,1)S(1)}, bf16[1024,2048]{1,0:T(8,128)(2,1)}, u32[]{:S(2)}) copy-start(bf16[1024,2048]{1,0:T(8,128)(2,1)} %wk_hbm.1) | copy-start | bytes 12582916
  3.0 1.0 %copy-start.1 = (bf16[128,2048]{1,0:T(8,128)(2,1)S(1)}, bf16[128,2048]{1,0:T(8,128)(2,1)}, u32[]{:S(2)}) copy-start(bf16[128,2048]{1,0:T(8,128)(2,1)} %q_ref.1) | copy-start | bytes 1572868
  4.0 1.0 %copy-start.2 = (bf16[32,8,1024]{2,1,0:T(8,128)(2,1)S(1)}, bf16[32,8,1024]{2,1,0:T(8,128)(2,1)}, u32[]{:S(2)}) copy-start(bf16[32,8,1024]{2,1,0:T(8,128)(2,1)} %param.7) | copy-start | bytes 1572868
  5.0 0.7 %copy-start.3 = (s32[2,2]{1,0:T(2,128)S(1)}, s32[2,2]{1,0:T(2,128)}, u32[]{:S(2)}) copy-start(s32[2,2]{1,0:T(2,128)} %ids_ref.1) | copy-start | bytes 52

commit v2 on v1

--- a/solution.py
+++ b/solution.py
@@ -88,11 +88,13 @@
     count,
     toks,
     ids_ref,
-    q_ref,
+    lengths_ref,
+    q_hbm,
     enc_hbm,
     wk_hbm,
     wv_hbm,
     out_ref,
+    q_ref,
     enc_ref,
     wk_ref,
     wv_ref,
@@ -102,7 +104,7 @@
     recv_buf,
     q_send,
     q_recv,
-    q_shift,
+    q_pairs,
     k_buf,
     v_buf,
     result,
@@ -122,7 +124,8 @@
     rows = 2 * toks
     total = count * rows
     enc_width = enc_ref.shape[1]
-    width = q_ref.shape[1]
+    tok_rows, width = q_ref.shape
+    half = count // 2
     offsets = sorted(range(1, count), reverse=True)
 
     def local(source, target, index):
@@ -148,6 +151,7 @@
             device_id={"seq": flipped(me, offset)},
             device_id_type=pl.DeviceIdType.MESH,
         )
+    q_load = local(q_hbm, q_ref, 3)
     enc_copy = local(enc_hbm, enc_ref, 0)
     wk_copy = local(wk_hbm, wk_ref, 1)
     wv_copy = local(wv_hbm, wv_ref, 2)
@@ -160,7 +164,8 @@
             mine = jnp.where(lane == me * 4 + span * 2 + which, value, mine)
     id_send[...] = mine
     id_recv[me] = mine
-    last = q_ref.shape[0] - 1
+    last = tok_rows - 1
+    q_load.wait()
     q_send[...] = q_ref[last - 15 :, :].astype(jnp.float32)[15:, :]
 
     pl.semaphore_wait(barrier, count - 1)
@@ -179,6 +184,18 @@
     ids = jnp.sum(id_recv[...], axis=0)
 
     x_copies = {}
+    own = pl.ds(pl.multiple_of(me * rows, rows), rows)
+    for slot in range(2):
+        for offset in offsets:
+            peer_at = flipped(me, offset)
+            theirs = pl.ds(pl.multiple_of(peer_at * rows, rows), rows)
+            x_copies[slot, offset] = remote(
+                send_buf.at[slot, theirs],
+                recv_buf.at[slot, own],
+                x_ssem.at[slot, offset],
+                x_rsem.at[slot, offset],
+                peer_at,
+            )
     for slot in range(2):
         row = lax.broadcasted_iota(jnp.int32, (total, 128), 0)
         lanes = lax.broadcasted_iota(jnp.int32, (total, 128), 1)
@@ -202,103 +219,141 @@
             send_buf[slot, :, cols] = jnp.dot(
                 pick, enc_ref[:, cols], preferred_element_type=jnp.float32
             ).astype(jnp.bfloat16)
-        own = pl.ds(pl.multiple_of(me * rows, rows), rows)
         for offset in offsets:
-            peer_at = flipped(me, offset)
-            theirs = pl.ds(pl.multiple_of(peer_at * rows, rows), rows)
-            copy = remote(
-                send_buf.at[slot, theirs],
-                recv_buf.at[slot, own],
-                x_ssem.at[slot, offset],
-                x_rsem.at[slot, offset],
-                peer_at,
-            )
-            copy.start()
-            x_copies[slot, offset] = copy
+            x_copies[slot, offset].start()
         recv_buf[slot, own, :] = send_buf[slot, own, :]
 
     q_copy.wait_recv()
+    blank = jnp.zeros((SPAN, DH), jnp.bfloat16)
     for part in range(width // 256):
         cols = slice(part * 256, part * 256 + 256)
         turned = pltpu.roll(q_ref[:, cols].astype(jnp.float32), 1, 0)
         first = lax.broadcasted_iota(jnp.int32, turned.shape, 0) == 0
         turned = jnp.where(first, jnp.broadcast_to(q_recv[:, cols], turned.shape), turned)
-        q_shift[:, cols] = turned.astype(jnp.bfloat16)
+        turned = turned.astype(jnp.bfloat16)
+        for slot in range(2):
+            span_rows = turned[slot * SPAN : slot * SPAN + SPAN, :]
+            q_pairs[slot, part, :SPAN, :DH] = span_rows[:, :DH]
+            q_pairs[slot, part, :SPAN, DH:] = blank
+            q_pairs[slot, part, SPAN:, :DH] = blank
+            q_pairs[slot, part, SPAN:, DH:] = span_rows[:, DH:]
     wk_copy.wait()
     wv_copy.wait()
 
-    scale = 1.0 / DH**0.5
+    near = total // 2
+    side = me // half
+    near_rows = pl.ds(pl.multiple_of(side * near, near), near)
+    far_rows = pl.ds(pl.multiple_of((1 - side) * near, near), near)
+
+    def project(slot, source, place, cols):
+        x = recv_buf[slot, source, :]
+        k_buf[slot, place, cols] = jnp.dot(
+            x, wk_ref[:, cols], preferred_element_type=jnp.float32
+        ).astype(jnp.bfloat16)
+        v_buf[slot, place, cols] = jnp.dot(
+            x, wv_ref[:, cols], preferred_element_type=jnp.float32
+        ).astype(jnp.bfloat16)
+
+    factor = 1.4426950408889634 / DH**0.5
+
+    def attend(slot, tile):
+        cols = slice(tile * 256, tile * 256 + 256)
+        scores = lax.dot_general(
+            k_buf[slot, :, cols],
+            q_pairs[slot, tile],
+            (((1,), (1,)), ((), ())),
+            preferred_element_type=jnp.float32,
+        )
+        top = jnp.max(scores, axis=0, keepdims=True)
+        expo = jnp.exp2((scores - top) * factor)
+        weights = (expo * (1.0 / jnp.sum(expo, axis=0, keepdims=True))).astype(jnp.bfloat16)
+        both = lax.dot_general(
+            weights,
+            v_buf[slot, :, cols],
+            (((0,), (0,)), ((), ())),
+            preferred_element_type=jnp.float32,
+        )
+        low = 7 + slot * SPAN
+        for part in range(2):
+            result[low : low + SPAN, tile * 256 + part * DH : tile * 256 + part * DH + DH] = both[
+                part * SPAN : part * SPAN + SPAN, part * DH : part * DH + DH
+            ]
+
+    room = tok_rows * count // lengths_ref.shape[0]
+    start = me * tok_rows
+    limit = lengths_ref[0]
+    for index in range(1, lengths_ref.shape[0]):
+        limit = jnp.where(start // room == index, lengths_ref[index], limit)
+
+    def finish(low, high):
+        within = start % room + low + lax.broadcasted_iota(jnp.int32, (high - low, 256), 0)
+        live = (within >= SPAN - 1) & (within < limit)
+        for part in range(width // 256):
+            cols = slice(part * 256, part * 256 + 256)
+            out_ref[low:high, cols] = jnp.where(
+                live, result[8 + low : 8 + high, cols], 0.0
+            ).astype(jnp.bfloat16)
+
     for slot in range(2):
         for offset in offsets:
-            x_copies[slot, offset].wait_recv()
+            if offset < half:
+                x_copies[slot, offset].wait_recv()
 
         @pl.loop(0, width // 256)
-        def project(tile):
-            cols = pl.ds(pl.multiple_of(tile * 256, 256), 256)
-            x = recv_buf[slot]
-            k_buf[:, cols] = jnp.dot(
-                x, wk_ref[:, cols], preferred_element_type=jnp.float32
-            ).astype(jnp.bfloat16)
-            v_buf[:, cols] = jnp.dot(
-                x, wv_ref[:, cols], preferred_element_type=jnp.float32
-            ).astype(jnp.bfloat16)
-
-        @pl.loop(0, HEADS // 4)
-        def attend(step):
-            for part in range(4):
-                cols = pl.ds(pl.multiple_of((step * 4 + part) * DH, DH), DH)
-                query = q_shift[slot * SPAN : slot * SPAN + SPAN, cols]
-                scores = (
-                    lax.dot_general(
-                        query,
-                        k_buf[:, cols],
-                        (((1,), (1,)), ((), ())),
-                        preferred_element_type=jnp.float32,
-                    )
-                    * scale
+        def project_near(tile):
+            project(
+                slot, near_rows, slice(0, near), pl.ds(pl.multiple_of(tile * 256, 256), 256)
+            )
+
+    for slot in range(2):
+        for offset in offsets:
+            if offset >= half:
+                x_copies[slot, offset].wait_recv()
+        tiles = width // 256
+        for tile in range(tiles + 1):
+            if tile < tiles:
+                project(
+                    slot, far_rows, slice(near, total), slice(tile * 256, tile * 256 + 256)
                 )
-                top = jnp.max(scores, axis=1, keepdims=True)
-                expo = jnp.exp(scores - top)
-                weights = (expo / jnp.sum(expo, axis=1, keepdims=True)).astype(jnp.bfloat16)
-                result[pl.ds(7 + slot * SPAN, SPAN), cols] = jnp.dot(
-                    weights, v_buf[:, cols], preferred_element_type=jnp.float32
-                )
-
+            if tile > 0:
+                attend(slot, tile - 1)
         if slot == 0:
             row_send[...] = result[7:8, :]
             row_copy = remote(row_send, row_recv, row_ssem.at[1], row_rsem.at[1], previous)
             row_copy.start()
+            finish(0, 48)
 
     row_copy.wait_recv()
     result[8 + last : 9 + last, :] = row_recv[...]
-    out_ref[...] = result[8 : 9 + last, :].astype(jnp.bfloat16)
+    finish(48, tok_rows)
     for offset in offsets:
         id_copies[offset].wait_send()
-        for slot in range(2):
-            x_copies[slot, offset].wait_send()
+        x_copies[0, offset].wait_send()
+        x_copies[1, offset].wait_send()
     q_copy.wait_send()
     row_copy.wait_send()
 
 
 def kernel_body(queries, encodings, neighbour_ids, lengths, w_key, w_value):
     count = lax.axis_size("seq")
-    position = lax.axis_index("seq")
     tok_rows, width = queries.shape
     held, toks, enc_width = encodings.shape
     total = count * 2 * toks
     dma = pltpu.SemaphoreType.DMA
-    attended = pl.pallas_call(
+    return pl.pallas_call(
         functools.partial(kernel, count, toks),
         out_shape=jax.ShapeDtypeStruct((tok_rows, width), jnp.bfloat16),
         in_specs=[
             pl.BlockSpec(memory_space=pltpu.SMEM),
-            pl.BlockSpec(memory_space=pltpu.VMEM),
+            pl.BlockSpec(memory_space=pltpu.SMEM),
+            pl.BlockSpec(memory_space=pl.ANY),
             pl.BlockSpec(memory_space=pl.ANY),
             pl.BlockSpec(memory_space=pl.ANY),
             pl.BlockSpec(memory_space=pl.ANY),
         ],
         out_specs=pl.BlockSpec(memory_space=pltpu.VMEM),
         scratch_shapes=[
+            pltpu.VMEM((tok_rows, width), jnp.bfloat16),
             pltpu.VMEM((held * toks, enc_width), jnp.bfloat16),
             pltpu.VMEM((enc_width, width), jnp.bfloat16),
             pltpu.VMEM((enc_width, width), jnp.bfloat16),
@@ -308,13 +363,13 @@
             pltpu.VMEM((2, total, enc_width), jnp.bfloat16),
             pltpu.VMEM((1, width), jnp.float32),
             pltpu.VMEM((1, width), jnp.float32),
-            pltpu.VMEM((tok_rows, width), jnp.bfloat16),
-            pltpu.VMEM((total, width), jnp.bfloat16),
-            pltpu.VMEM((total, width), jnp.bfloat16),
+            pltpu.VMEM((2, width // 256, 2 * SPAN, 256), jnp.bfloat16),
+            pltpu.VMEM((2, total, width), jnp.bfloat16),
+            pltpu.VMEM((2, total, width), jnp.bfloat16),
             pltpu.VMEM((tok_rows + 8, width), jnp.float32),
             pltpu.VMEM((1, width), jnp.float32),
             pltpu.VMEM((1, width), jnp.float32),
-            dma((3,)),
+            dma((4,)),
             dma((count,)),
             dma((count,)),
             dma((2, count)),
@@ -323,26 +378,12 @@
             dma((2,)),
         ],
         compiler_params=pltpu.CompilerParams(
-            collective_id=0, has_side_effects=True, vmem_limit_bytes=48 * 1024 * 1024
+            collective_id=0, has_side_effects=True, vmem_limit_bytes=62 * 1024 * 1024
         ),
         cost_estimate=pl.CostEstimate(
             flops=8 * total * enc_width * width, bytes_accessed=10 << 20, transcendentals=0
         ),
-    )(neighbour_ids, queries, encodings.reshape(held * toks, enc_width), w_key, w_value)
-    slot_room = tok_rows * count // lengths.shape[0]
-    global_rows = position * tok_rows + jnp.arange(tok_rows, dtype=jnp.int32)
-    within = global_rows % slot_room
-    prompt = global_rows // slot_room
-    limit = jnp.sum(
-        jnp.where(
-            prompt[:, None] == jnp.arange(lengths.shape[0], dtype=jnp.int32)[None, :],
-            lengths[None, :],
-            0,
-        ),
-        axis=1,
-    )
-    live = (within >= 63) & (within < limit)
-    return jnp.where(live[:, None], attended, 0).astype(jnp.bfloat16)
+    )(neighbour_ids, lengths, queries, encodings.reshape(held * toks, enc_width), w_key, w_value)
 
 
 def body(queries, encodings, neighbour_ids, lengths, w_key, w_value):
@@ -350,7 +391,9 @@
     held, toks, enc_width = encodings.shape
     small = count <= 32 and count & (count - 1) == 0 and held <= 256
     tiled = (2 * toks) % 16 == 0 and (held * toks) % 16 == 0
-    if small and tiled and queries.shape[0] == 2 * SPAN:
+    room = 2 * SPAN * count // lengths.shape[0]
+    whole = room % (2 * SPAN) == 0
+    if small and tiled and whole and queries.shape[0] == 2 * SPAN:
         return kernel_body(queries, encodings, neighbour_ids, lengths, w_key, w_value)
     return general_body(queries, encodings, neighbour_ids, lengths, w_key, w_value)
 

time: 56.5 us -> 42.9 us (0.76)
  Pallas kernels: 49.6 us -> 40.8 us
  local copies, waits for them, and re-layouts: 4.94 us -> 1.88 us
  other arithmetic: 1.67 us -> 0 us
    pallas_call x1, Pallas kernels: 49.6 us -> 40.8 us  [kernel_body(): pl.pallas_call(functools.partial(kernel, count, toks), out_shape=jax.Shap...]
    unnamed x8 -> x1, local copies, waits for them, and re-layouts: 4.94 us -> 1.88 us
    select_n x2 -> x0, other arithmetic: 0.91 us -> none  [the longest x1 0.9 us: kernel_body(): return jnp.where(live[:, None], attended, 0).astype(jnp.bfloat16)]
    reduce_sum x1 -> x0, other arithmetic: 0.74 us -> none  [kernel_body(): jnp.sum(jnp.where(prompt[:, None] == jnp.arange(lengths.shape[0], dtype=j...]
where the time goes in v2:
time: 42.9 us; the launch traced here: 42.7 us
  Pallas kernels  40.8 us (95%)
  local copies, waits for them, and re-layouts  1.88 us (4%)
    pallas_call x1, Pallas kernels, kernel_body(): pl.pallas_call(functools.partial(kernel, count, toks), out_shape=jax.Shap...  40.8 us
    unnamed x1, local copies, waits for them, and re-layouts  1.88 us

profile of v2, /device:TPU:0, one launch (start us, length us, event | category | flops | bytes accessed | tf_op | source)
XLA Modules:
  0.0 42.7 jit_solution(9906688912929024261)
XLA Ops:
  0.0 40.8 %shard_map.64 = bf16[128,2048]{1,0:T(8,128)(2,1)} custom-call(s32[2,2]{1,0:T(2,128)} %ids_ref.1, s32[2]{0:T(128)} %lengths_ref.1, bf16[128,2048]{1,0:T(8,128)(2,1)} %q_hbm.1, bf16[256,1024]{1,0:T(8,128)(2,1)} %bitcast.1, bf16[1024,2048]{1,0:T(8,128)(2,1)} %wk_hbm.1, bf16[1024,2048]{1,0:T(8,128)(2,1)} %wv_hbm.1), custom_call_target="tpu_custom_call" | custom-call | flops 4294967296 | bytes 10485760 | tf_op jit(solution)/shard_map/pallas_call | solution.py:343
  40.8 1.9 %copy.8 = bf16[128,2048]{1,0:T(8,128)(2,1)} copy(bf16[128,2048]{1,0:T(8,128)(2,1)} %shard_map.64) | data formatting | bytes 1048576

commit v3 on v2

--- a/solution.py
+++ b/solution.py
@@ -93,6 +93,7 @@
     enc_hbm,
     wk_hbm,
     wv_hbm,
+    out_hbm,
     out_ref,
     q_ref,
     enc_ref,
@@ -117,6 +118,7 @@
     x_rsem,
     row_ssem,
     row_rsem,
+    out_sem,
 ):
     me = lax.axis_index("seq")
     following = lax.rem(me + 1, count)
@@ -220,8 +222,14 @@
                 pick, enc_ref[:, cols], preferred_element_type=jnp.float32
             ).astype(jnp.bfloat16)
         for offset in offsets:
-            x_copies[slot, offset].start()
+            if offset >= half:
+                x_copies[slot, offset].start()
         recv_buf[slot, own, :] = send_buf[slot, own, :]
+
+    for slot in range(2):
+        for offset in offsets:
+            if offset < half:
+                x_copies[slot, offset].start()
 
     q_copy.wait_recv()
     blank = jnp.zeros((SPAN, DH), jnp.bfloat16)
@@ -285,14 +293,23 @@
     for index in range(1, lengths_ref.shape[0]):
         limit = jnp.where(start // room == index, lengths_ref[index], limit)
 
-    def finish(low, high):
+    tiles = width // 256
+    out_copies = []
+
+    def finish(low, high, first, stop):
         within = start % room + low + lax.broadcasted_iota(jnp.int32, (high - low, 256), 0)
         live = (within >= SPAN - 1) & (within < limit)
-        for part in range(width // 256):
+        for part in range(first, stop):
             cols = slice(part * 256, part * 256 + 256)
             out_ref[low:high, cols] = jnp.where(
                 live, result[8 + low : 8 + high, cols], 0.0
             ).astype(jnp.bfloat16)
+        block = (slice(low, high), slice(first * 256, stop * 256))
+        copy = pltpu.make_async_copy(
+            out_ref.at[block], out_hbm.at[block], out_sem.at[len(out_copies)]
+        )
+        copy.start()
+        out_copies.append(copy)
 
     for slot in range(2):
         for offset in offsets:
@@ -309,29 +326,32 @@
         for offset in offsets:
             if offset >= half:
                 x_copies[slot, offset].wait_recv()
-        tiles = width // 256
-        for tile in range(tiles + 1):
+        for tile in range(tiles + 2):
             if tile < tiles:
                 project(
                     slot, far_rows, slice(near, total), slice(tile * 256, tile * 256 + 256)
                 )
-            if tile > 0:
+            if 0 < tile <= tiles:
                 attend(slot, tile - 1)
+            if slot == 1 and tile > 1:
+                finish(48, tok_rows - 16, tile - 2, tile - 1)
         if slot == 0:
             row_send[...] = result[7:8, :]
             row_copy = remote(row_send, row_recv, row_ssem.at[1], row_rsem.at[1], previous)
             row_copy.start()
-            finish(0, 48)
+            finish(0, 48, 0, tiles)
 
     row_copy.wait_recv()
     result[8 + last : 9 + last, :] = row_recv[...]
-    finish(48, tok_rows)
+    finish(tok_rows - 16, tok_rows, 0, tiles)
     for offset in offsets:
         id_copies[offset].wait_send()
         x_copies[0, offset].wait_send()
         x_copies[1, offset].wait_send()
     q_copy.wait_send()
     row_copy.wait_send()
+    for copy in out_copies:
+        copy.wait()
 
 
 def kernel_body(queries, encodings, neighbour_ids, lengths, w_key, w_value):
@@ -351,8 +371,9 @@
             pl.BlockSpec(memory_space=pl.ANY),
             pl.BlockSpec(memory_space=pl.ANY),
         ],
-        out_specs=pl.BlockSpec(memory_space=pltpu.VMEM),
+        out_specs=pl.BlockSpec(memory_space=pl.ANY),
         scratch_shapes=[
+            pltpu.VMEM((tok_rows, width), jnp.bfloat16),
             pltpu.VMEM((tok_rows, width), jnp.bfloat16),
             pltpu.VMEM((held * toks, enc_width), jnp.bfloat16),
             pltpu.VMEM((enc_width, width), jnp.bfloat16),
@@ -376,6 +397,7 @@
             dma((2, count)),
             dma((2,)),
             dma((2,)),
+            dma((width // 256 + 2,)),
         ],
         compiler_params=pltpu.CompilerParams(
             collective_id=0, has_side_effects=True, vmem_limit_bytes=62 * 1024 * 1024

time: 42.9 us -> 42.7 us (level)
  no operation moved by 1% of the time
where the time goes in v3:
time: 42.7 us; the launch traced here: 42.5 us
  Pallas kernels  40.6 us (95%)
  local copies, waits for them, and re-layouts  1.88 us (4%)
    pallas_call x1, Pallas kernels, kernel_body(): pl.pallas_call(functools.partial(kernel, count, toks), out_shape=jax.Shap...  40.6 us
    unnamed x1, local copies, waits for them, and re-layouts  1.88 us

profile of v3, /device:TPU:0, one launch (start us, length us, event | category | flops | bytes accessed | tf_op | source)
XLA Modules:
  0.0 42.5 jit_solution(1151734539992714192)
XLA Ops:
  0.0 40.6 %shard_map.64 = bf16[128,2048]{1,0:T(8,128)(2,1)} custom-call(s32[2,2]{1,0:T(2,128)} %ids_ref.1, s32[2]{0:T(128)} %lengths_ref.1, bf16[128,2048]{1,0:T(8,128)(2,1)} %q_hbm.1, bf16[256,1024]{1,0:T(8,128)(2,1)} %bitcast.1, bf16[1024,2048]{1,0:T(8,128)(2,1)} %wk_hbm.1, bf16[1024,2048]{1,0:T(8,128)(2,1)} %wv_hbm.1), custom_call_target="tpu_custom_call" | custom-call | flops 4294967296 | bytes 10485760 | tf_op jit(solution)/shard_map/pallas_call | solution.py:363
  40.6 1.9 %copy.8 = bf16[128,2048]{1,0:T(8,128)(2,1)} copy(bf16[128,2048]{1,0:T(8,128)(2,1)} %shard_map.64) | data formatting | bytes 1048576
